TPU v7x, 32 devices: a whole 2x2x4 slice. The times are simulated.
32 devices in a mesh: ctx: 8 (over z, x), head: 4 (over y, core).
Axes of the slice: x: 2, y: 2, z: 4, core: 2. Of those that a mesh axis runs over, the one named last changes fastest.
Arguments:
- queries: bfloat16 [2048, 2048], P('ctx', 'head'), may hold values from -110 to 110
- keys: bfloat16 [32768, 128], P('ctx'), may hold values from -6 to 6
- values: bfloat16 [32768, 128], P('ctx'), may hold values from -6 to 6
- w_out: bfloat16 [2048, 16384], P(None, 'head'), may hold values from -0.125 to 0.125
- new_counts: int32 [8], replicated, may hold values from 1 to 1024, as said below
- prior_lengths: int32 [8], replicated, may hold values from 1 to 15360, as said below
Outputs:
- mixed: bfloat16 [2048, 16384], P('ctx', 'head')
Inputs may be any that keep to these rules, and one draw needn't show every extreme that they name: `new_counts`: every request has at least one new token; the counts add up to 2048. `prior_lengths`: every request has at least one cached token; the lengths add up to 30720.
All inputs are finite; a program needn't handle non-finite values.
Results may differ from a plain program's by a relative error of at most 0.011.
Values may be sent and summed in bfloat16 or wider, within the bound.
No kernel may reach another device: no remote copies, remote signals or barrier semaphores. Data moves between devices by JAX's collectives and lax.ppermute only.
A program may use at most 384 MiB of HBM per device.

v0:
```python
import functools
import math

import jax
import jax.numpy as jnp
from jax import lax
from jax.experimental import pallas as pl
from jax.experimental.pallas import tpu as pltpu
from jax.sharding import PartitionSpec as P

NEG = -1e30
CALM = 60.0
KEY_TILE = 512
FEW_ROWS = 64
SIDE = 16
SLACK = 1.05
LANES = 128
MIB = 1024 * 1024
SMEM = pl.BlockSpec(memory_space=pltpu.SMEM)
VMEM = pl.BlockSpec(memory_space=pltpu.VMEM)
HBM = pl.BlockSpec(memory_space=pltpu.HBM)


def lengths(rows):
    wide = rows.astype(jnp.float32)
    ones = jnp.ones((rows.shape[1], LANES), jnp.bfloat16)
    return jnp.dot((wide * wide).astype(jnp.bfloat16), ones, preferred_element_type=jnp.float32)


def fill(parts, keys_ref, beside_ref):
    width = keys_ref.shape[1]
    longest = jnp.zeros((KEY_TILE, LANES), jnp.float32)
    for from_keys, from_values, done in parts:
        step = min(KEY_TILE, from_keys.shape[0])

        def turn(at, longest, from_keys=from_keys, from_values=from_values, done=done, step=step):
            here = pl.ds(pl.multiple_of(at * step, step), step)
            there = pl.ds(pl.multiple_of(done + at * step, step), step)
            keys = from_keys[here, :]
            keys_ref[there, :] = keys
            beside_ref[there, :width] = from_values[here, :]
            beside_ref[there, width:] = jnp.ones((step, width), jnp.bfloat16)
            return jnp.maximum(longest, lengths(keys))

        longest = lax.fori_loop(0, from_keys.shape[0] // step, turn, longest)
    return jnp.max(longest)


def prepare_kernel(keys_ref, values_ref, far_w, all_keys, beside_ref, longest_ref, near_w, sem):
    fetch = pltpu.make_async_copy(far_w, near_w, sem)
    fetch.start()
    longest_ref[0] = fill([(keys_ref, values_ref, 0)], all_keys, beside_ref)
    fetch.wait()


def prepare(keys, values, w_out):
    cache, width = keys.shape
    return pl.pallas_call(
        prepare_kernel,
        out_shape=(
            pltpu.VMEM((2 * cache, width), jnp.bfloat16),
            pltpu.VMEM((2 * cache, 2 * width), jnp.bfloat16),
            jax.ShapeDtypeStruct((1,), jnp.float32),
            pltpu.VMEM(w_out.shape, w_out.dtype),
        ),
        in_specs=[VMEM, VMEM, HBM],
        out_specs=(VMEM, VMEM, SMEM, VMEM),
        scratch_shapes=[pltpu.SemaphoreType.DMA],
        compiler_params=pltpu.CompilerParams(vmem_limit_bytes=4 * MIB),
        name="prepare",
    )(keys, values, pltpu.with_memory_space_constraint(w_out, pltpu.HBM))


def join_kernel(got_ref, rest_ref, own_ref, keys_in, beside_in, all_keys, beside_ref, longest_ref):
    del keys_in, beside_in
    half, width = got_ref.shape[0], all_keys.shape[1]
    parts = [
        (ref.at[:, :width], ref.at[:, width:], 2 * half + at * half) for at, ref in enumerate((got_ref, rest_ref))
    ]
    longest_ref[0] = jnp.maximum(own_ref[0], fill(parts, all_keys, beside_ref))


def join(got, rest, own_longest, all_keys, beside):
    return pl.pallas_call(
        join_kernel,
        out_shape=(
            pltpu.VMEM(all_keys.shape, all_keys.dtype),
            pltpu.VMEM(beside.shape, beside.dtype),
            jax.ShapeDtypeStruct((1,), jnp.float32),
        ),
        in_specs=[VMEM, VMEM, SMEM, VMEM, VMEM],
        out_specs=(VMEM, VMEM, SMEM),
        input_output_aliases={3: 0, 4: 1},
        compiler_params=pltpu.CompilerParams(vmem_limit_bytes=4 * MIB),
        name="join",
    )(got, rest, own_longest, all_keys, beside)


def stack_kernel(slots, group_at, width, plan_ref, *refs):
    q_refs, (stack_ref, longest_ref, q_all, sems) = refs[:slots], refs[slots:]
    rows = q_refs[0].shape[0]
    heads = q_refs[0].shape[1] // width
    local = slots * rows
    copies = [pltpu.make_async_copy(q_ref, q_all.at[slot], sems.at[slot]) for slot, q_ref in enumerate(q_refs)]
    for copy in copies:
        copy.start()
    longest = jnp.zeros((rows, LANES), jnp.float32)
    for slot, copy in enumerate(copies):
        copy.wait()
        start = plan_ref[group_at + slot] * rows
        for head in range(heads):
            part = q_all[slot, :, head * width:(head + 1) * width]
            stack_ref[pl.ds(pl.multiple_of(head * local + start, rows), rows), :] = part
            longest = jnp.maximum(longest, lengths(part))
    longest_ref[0] = jnp.max(longest)


def stack_queries(places, plan, queries, width):
    slots, (rows, wide) = len(queries), queries[0].shape
    return pl.pallas_call(
        functools.partial(stack_kernel, slots, places["groups"], width),
        out_shape=(
            pltpu.VMEM((slots * rows * (wide // width), width), jnp.bfloat16),
            jax.ShapeDtypeStruct((1,), jnp.float32),
        ),
        in_specs=[SMEM] + [HBM] * slots,
        out_specs=(VMEM, SMEM),
        scratch_shapes=[pltpu.VMEM((slots, rows, wide), jnp.bfloat16), pltpu.SemaphoreType.DMA((slots,))],
        compiler_params=pltpu.CompilerParams(vmem_limit_bytes=4 * MIB),
        name="stack",
    )(plan, *queries)


def request_table(new_ref, prior_ref):
    table = []
    row, key = jnp.int32(0), jnp.int32(0)
    for request in range(new_ref.shape[0]):
        new, prior = new_ref[request], prior_ref[request]
        table.append((row, key, key + prior - row, row + new, key + new + prior))
        row, key = row + new, key + new + prior
    return table


def key_range(table, row):
    first, shift = table[0][1], table[0][2]
    for start, key, ahead, _, _ in table[1:]:
        own = row >= start
        first = jnp.where(own, key, first)
        shift = jnp.where(own, ahead, shift)
    return first, row + shift


def attend_kernel(shape, places, first_head, heads, *refs):
    groups, rows, requests, many = shape
    plan_ref, key_norm_ref, query_norm_ref, stack_ref, keys_ref, beside_ref = refs[:6]
    out_refs = refs[6:6 + groups]
    sums, tops, chunk_q, chunk_sum, chunk_top = refs[6 + groups:]
    width = keys_ref.shape[1]
    local = groups * rows
    step = min(KEY_TILE, keys_ref.shape[0] // 4)
    scale = width ** (-0.5)
    factor = scale * math.log2(math.e)
    calm = key_norm_ref[0] * query_norm_ref[0] * (SLACK * scale * scale) <= CALM * CALM
    side = plan_ref[places["side"]]

    def clear(at, carry):
        sums[pl.ds(pl.multiple_of(at * rows, rows), rows), :] = jnp.zeros((rows, 2 * width), jnp.float32)
        return carry

    lax.fori_loop(0, heads * groups, clear, 0)

    def global_row(place):
        whole = place + side * rows
        for group in range(1, groups):
            whole = whole + jnp.where(place >= group * rows, rows, 0)
        return whole

    def one_chunk(count, online, request, begin, end, start):
        first_key = plan_ref[places["first_key"] + request]
        ahead = plan_ref[places["ahead"] + request]
        start = pl.multiple_of(start, SIDE)
        low_key, high_key = global_row(begin) + ahead, global_row(end - 1) + ahead
        total = heads * count
        for head in range(heads):
            chunk_q[head * count:(head + 1) * count, :] = stack_ref[
                pl.ds(pl.multiple_of((first_head + head) * local + start, SIDE), count), :
            ]
        chunk_sum[:total, :] = jnp.zeros((total, 2 * width), jnp.float32)
        if online:
            chunk_top[:total, :] = jnp.full((total, width), NEG, jnp.float32)
        place = start + lax.broadcasted_iota(jnp.int32, (count, 1), 0)
        last = global_row(place) + ahead

        def scores(part, left):
            return lax.dot_general(
                chunk_q[part, :], keys_ref[pl.ds(left, step), :], (((1,), (1,)), ((), ())),
                preferred_element_type=jnp.float32,
            ) * factor

        def add(left, weights):
            return jnp.dot(
                weights.astype(jnp.bfloat16), beside_ref[pl.ds(left, step), :], preferred_element_type=jnp.float32
            )

        def one_step(left, key):
            def allowed():
                index = key + lax.broadcasted_iota(jnp.int32, (count, step), 1)
                return (index >= first_key) & (index <= last)

            if online:
                mask = allowed()

                def one_head(head, carry):
                    part = pl.ds(pl.multiple_of(head * count, count), count)
                    score = jnp.where(mask, scores(part, left), NEG)
                    old = chunk_top[part, :]
                    new = jnp.maximum(old, jnp.ceil(jnp.max(score, axis=1, keepdims=True)))
                    weights = jnp.where(mask, jnp.exp2(score - new[:, :1]), 0.0)
                    shrink = jnp.exp2(old - new)
                    chunk_sum[part, :width] = chunk_sum[part, :width] * shrink
                    chunk_sum[part, width:] = chunk_sum[part, width:] * shrink
                    chunk_sum[part, :] += add(left, weights)
                    chunk_top[part, :] = new
                    return carry

                lax.fori_loop(0, heads, one_head, 0)
                return

            plain = (key >= first_key) & (key + step - 1 <= low_key)

            @pl.when(plain)
            def _():
                chunk_sum[:total, :] += add(left, jnp.exp2(scores(pl.ds(0, total), left)))

            @pl.when(jnp.logical_not(plain))
            def _():
                mask = allowed()
                weights = jnp.exp2(scores(pl.ds(0, total), left))
                weights = jnp.concatenate([
                    jnp.where(mask, weights[head * count:(head + 1) * count, :], 0.0) for head in range(heads)
                ])
                chunk_sum[:total, :] += add(left, weights)

        def one_part(part, carry):
            left, key, steps = (plan_ref[places[name] + part] for name in ("lefts", "keys", "steps"))
            low = jnp.clip(lax.div(first_key - key, step), 0, steps)
            high = jnp.clip(lax.div(high_key - key + step, step), 0, steps)

            def turn(at, carry):
                one_step(pl.multiple_of(left + at * step, step), key + at * step)
                return carry

            lax.fori_loop(low, high, turn, 0)
            return carry

        lax.fori_loop(0, 3, one_part, 0)
        own = (place >= begin) & (place < end)
        for head in range(heads):
            here = pl.ds(pl.multiple_of(head * local + start, SIDE), count)
            part = slice(head * count, (head + 1) * count)
            sums[here, :] += jnp.where(own, chunk_sum[part, :], 0.0)
            if online:
                tops[here, :] = jnp.where(own, chunk_top[part, :], tops[here, :])

    def all_chunks(count, online, request, begin, end):
        aligned = lax.div(begin, SIDE) * SIDE

        def turn(at, carry):
            from_row = aligned + at * count
            one_chunk(
                count,
                online,
                request,
                jnp.maximum(begin, from_row),
                jnp.minimum(end, from_row + count),
                jnp.minimum(from_row, local - count),
            )
            return carry

        lax.fori_loop(0, lax.div(end - aligned + (count - 1), count), turn, 0)

    few = min(FEW_ROWS, local)

    def one_request(request, carry):
        begin, end = plan_ref[places["begin"] + request], plan_ref[places["end"] + request]
        large = end - lax.div(begin, SIDE) * SIDE > 2 * few

        @pl.when((end > begin) & calm & large)
        def _():
            all_chunks(many, False, request, begin, end)

        @pl.when((end > begin) & calm & jnp.logical_not(large))
        def _():
            all_chunks(few, False, request, begin, end)

        @pl.when((end > begin) & jnp.logical_not(calm))
        def _():
            all_chunks(few, True, request, begin, end)

        return carry

    lax.fori_loop(0, requests, one_request, 0)

    lane = lax.broadcasted_iota(jnp.int32, (LANES, LANES), 1)
    for slot, out_ref in enumerate(out_refs):
        start = plan_ref[places["groups"] + slot] * rows
        if heads * width > rows:
            out_ref[rows:, :] = jnp.zeros((out_ref.shape[0] - rows, heads * width), jnp.bfloat16)
        for at in range(0, rows, LANES):
            terms = jnp.zeros((LANES, LANES), jnp.float32)
            for head in range(heads):
                here = pl.ds(pl.multiple_of(head * local + start + at, LANES), LANES)
                out_ref[at:at + LANES, head * width:(head + 1) * width] = sums[here, :width].astype(jnp.bfloat16)
                weight = sums[here, width:]
                top = jnp.where(weight > 0.0, jnp.where(calm, 0.0, tops[here, :]), NEG)
                for term, value in enumerate((weight, top)):
                    high = value.astype(jnp.bfloat16).astype(jnp.float32)
                    terms = jnp.where(lane == 2 * term * heads + head, high, terms)
                    terms = jnp.where(lane == (2 * term + 1) * heads + head, value - high, terms)
            fold, column = at // (heads * width), at % (heads * width)
            out_ref[rows + fold * SIDE:rows + (fold + 1) * SIDE, column:column + LANES] = terms.T[:SIDE, :].astype(
                jnp.bfloat16
            )


def side_rows(rows, wide):
    return SIDE * max(1, rows // wide)


def attend(places, plan, norms, stack, keys, beside, shape, first_head, heads):
    groups, rows, _ = shape
    width = keys.shape[1]
    local, wide = groups * rows, heads * width
    many = min(2 * rows + SIDE, local)
    return pl.pallas_call(
        functools.partial(attend_kernel, (*shape, many), dict(places), first_head, heads),
        out_shape=(jax.ShapeDtypeStruct((rows + side_rows(rows, wide), wide), jnp.bfloat16),) * groups,
        in_specs=[SMEM] * 3 + [VMEM] * 3,
        out_specs=(VMEM,) * groups,
        scratch_shapes=[
            pltpu.VMEM((heads * local, 2 * width), jnp.float32),
            pltpu.VMEM((heads * local, width), jnp.float32),
            pltpu.VMEM((heads * many, width), jnp.bfloat16),
            pltpu.VMEM((heads * many, 2 * width), jnp.float32),
            pltpu.VMEM((heads * min(FEW_ROWS, local), width), jnp.float32),
        ],
        compiler_params=pltpu.CompilerParams(vmem_limit_bytes=20 * MIB),
        cost_estimate=pl.CostEstimate(
            flops=local * heads * keys.shape[0] * width * 2, bytes_accessed=8 * MIB, transcendentals=0
        ),
        name="attend",
    )(plan, *norms, stack, keys, beside)


def merge_kernel(heads, there_at, plan_ref, *refs):
    parts, out_ref = refs[:-1], refs[-1]
    rows = out_ref.shape[0]
    width = out_ref.shape[1] // heads
    logs = [
        jnp.where(
            plan_ref[there_at + at] == 1,
            jnp.concatenate([
                part[row:row + SIDE, :min(rows, out_ref.shape[1])] for row in range(rows, part.shape[0], SIDE)
            ], axis=1).astype(jnp.float32),
            0.0,
        )
        for at, part in enumerate(parts)
    ]
    spare = LANES - SIDE * len(parts)
    if spare:
        logs.append(jnp.zeros((spare, rows), jnp.float32))
    terms = jnp.concatenate(logs, axis=0).T
    total = terms + pltpu.roll(terms, LANES - heads, 1)
    top = pltpu.roll(terms, LANES - 2 * heads, 1) + pltpu.roll(terms, LANES - 3 * heads, 1)
    lane = lax.broadcasted_iota(jnp.int32, (rows, LANES), 1)
    used = (lax.rem(lane, SIDE) < heads) & (lane < SIDE * len(parts)) & (total > 0.0)
    top = jnp.where(used, top, NEG)
    biggest = top
    for shift in (16, 32, 64):
        biggest = jnp.maximum(biggest, pltpu.roll(biggest, shift, 1))
    share = jnp.where(used, jnp.exp2(top - biggest), 0.0)
    weight = share * jnp.where(used, total, 0.0)
    for shift in (16, 32, 64):
        weight = weight + pltpu.roll(weight, shift, 1)
    share = share / weight
    for head in range(heads):
        own = slice(head * width, (head + 1) * width)
        mixed = jnp.zeros((rows, width), jnp.float32)
        for at, part in enumerate(parts):
            lane_at = at * SIDE + head
            mixed = mixed + part[:rows, own].astype(jnp.float32) * share[:, lane_at:lane_at + 1]
        out_ref[:, own] = mixed.astype(out_ref.dtype)


def merge(places, plan, parts, rows, heads):
    return pl.pallas_call(
        functools.partial(merge_kernel, heads, places["there"]),
        out_shape=jax.ShapeDtypeStruct((rows, parts[0].shape[1]), jnp.bfloat16),
        in_specs=[SMEM] + [VMEM] * len(parts),
        out_specs=VMEM,
        compiler_params=pltpu.CompilerParams(vmem_limit_bytes=12 * MIB),
        name="merge",
    )(plan, *parts)


def project_kernel(pieces, parts, part, from_at, plan_ref, *refs):
    refs = list(refs)
    before_ref = refs.pop(0) if part else None
    piece_refs, (w_ref, out_ref, token_ref) = refs[:pieces], refs[pieces:]
    token_ref[0] = jnp.int32(part)
    deep = piece_refs[0].shape[1]
    block = out_ref.shape[1]
    left = pl.multiple_of(pl.program_id(0) * block, block)
    total = None
    for at, piece_ref in enumerate(piece_refs):
        own = pl.multiple_of((plan_ref[from_at + at] * parts + part) * deep, deep)
        term = jnp.dot(
            piece_ref[...], w_ref[pl.ds(own, deep), pl.ds(left, block)], preferred_element_type=jnp.float32
        )
        total = term if total is None else total + term
    if part:
        total = total + before_ref[:, pl.ds(left, block)]
    out_ref[...] = total.astype(out_ref.dtype)


def project(places, plan, pieces, parts, part, before, w_out):
    rows, deep = pieces[0].shape
    depth, wide = w_out.shape
    block = min(1024, wide)
    last = part == parts - 1
    return pl.pallas_call(
        functools.partial(project_kernel, len(pieces), parts, part, places["from"]),
        out_shape=(
            pltpu.HBM((rows, wide), jnp.bfloat16) if last else pltpu.VMEM((rows, wide), jnp.float32),
            jax.ShapeDtypeStruct((1,), jnp.int32),
        ),
        grid=(wide // block,),
        in_specs=[SMEM] + [VMEM] * (bool(part) + len(pieces) + 1),
        out_specs=(pl.BlockSpec((rows, block), lambda at: (0, at)), SMEM),
        compiler_params=pltpu.CompilerParams(vmem_limit_bytes=16 * MIB),
        cost_estimate=pl.CostEstimate(
            flops=2 * rows * depth * wide // parts, bytes_accessed=2 * depth * wide // parts, transcendentals=0
        ),
        name="project",
    )(plan, *([before] if part else []), *pieces, w_out)


def shift_pairs(count, stride, steps):
    groups = count // stride
    return [
        (group * stride + member, (group + steps) % groups * stride + member)
        for group in range(groups)
        for member in range(stride)
    ]


def swap_pairs(count):
    return [(at, at ^ 1) for at in range(count)]


def is_far(groups, one, two):
    low, high = min(one, two), max(one, two)
    return low < groups // 2 and high >= groups - max(1, groups // 4)


def move(value, groups, steps, far):
    pairs = [
        (source, target)
        for source, target in shift_pairs(2 * groups, 2, steps)
        if far or not is_far(groups, source // 2, target // 2)
    ]
    return lax.ppermute(value, "ctx", pairs) if pairs else jnp.zeros_like(value)


def plan_kernel(shape, places, new_ref, prior_ref, at_ref, plan_ref, far_ref):
    groups, chips, rows, cache, step = shape
    device, place = at_ref[0], at_ref[1]
    group, side, chip, core = lax.div(device, 2), lax.rem(device, 2), lax.div(place, 2), lax.rem(place, 2)
    table = request_table(new_ref, prior_ref)

    def rows_before(row):
        block = lax.div(row, rows)
        odd, inside = lax.rem(block, 2), lax.rem(row, rows)
        return lax.div(block, 2) * rows + jnp.where(odd == side, inside, jnp.where(odd == 1, rows, 0))

    for request, (row, key, ahead, row_end, _) in enumerate(table):
        plan_ref[places["first_key"] + request] = key
        plan_ref[places["ahead"] + request] = ahead
        plan_ref[places["begin"] + request] = rows_before(row)
        plan_ref[places["end"] + request] = rows_before(row_end)
    spans = [
        (key_range(table, jnp.int32(2 * rows * at))[0], key_range(table, jnp.int32(2 * rows * (at + 1) - 1))[1])
        for at in range(groups)
    ]
    needed = jnp.int32(0)
    for source in range(groups):
        for target in range(groups):
            if is_far(groups, source, target):
                first, last = spans[source]
                meet = (first < 2 * cache * (target + 1)) & (last >= 2 * cache * target)
                needed = jnp.where(meet, 1, needed)
    far_ref[0] = needed
    plan_ref[places["side"]] = side
    for steps in range(groups):
        plan_ref[places["groups"] + steps] = lax.rem(group + (groups - steps), groups)
        there = jnp.int32(1)
        for at in range(groups):
            if is_far(groups, (at + steps) % groups, at):
                there = jnp.where(group == at, needed, there)
        plan_ref[places["there"] + steps] = there
    other = (device + 1 - 2 * side) * cache
    half = cache // 2
    stretches = [(0, device * cache, cache), (cache, other + core * half, half), (cache + half, other + (1 - core) * half, half)]
    for part, (left, key, count) in enumerate(stretches):
        plan_ref[places["lefts"] + part] = jnp.int32(left)
        plan_ref[places["keys"] + part] = key
        plan_ref[places["steps"] + part] = jnp.int32(count // step)
    for at in range(2 * chips):
        own = core if at < chips else 1 - core
        plan_ref[places["from"] + at] = lax.rem(chip + (chips - at % chips), chips) * 2 + own


def make_plan(shape, new_counts, prior_lengths, at):
    groups, chips = shape[:2]
    requests = new_counts.shape[0]
    sizes = dict(first_key=requests, ahead=requests, begin=requests, end=requests, side=1)
    sizes.update(groups=groups, there=groups, lefts=3, keys=3, steps=3)
    sizes["from"] = 2 * chips
    places, total = {}, 0
    for name, size in sizes.items():
        places[name] = total
        total += size
    plan, far = pl.pallas_call(
        functools.partial(plan_kernel, shape, dict(places)),
        out_shape=(jax.ShapeDtypeStruct((total,), jnp.int32), jax.ShapeDtypeStruct((1,), jnp.int32)),
        in_specs=[SMEM] * 3,
        out_specs=(SMEM, SMEM),
        name="plan",
    )(new_counts, prior_lengths, at)
    return places, plan, far


def body(queries, keys, values, w_out, new_counts, prior_lengths):
    ctx_count, head_count = lax.axis_size("ctx"), lax.axis_size("head")
    rows = queries.shape[0]
    cache = keys.shape[0]
    groups, chips = ctx_count // 2, head_count // 2
    at = jnp.stack([lax.axis_index("ctx"), lax.axis_index("head")]).astype(jnp.int32)
    shape = (groups, chips, rows, cache, min(KEY_TILE, cache // 2))
    places, plan, far = make_plan(shape, new_counts, prior_lengths, at)
    requests = new_counts.shape[0]
    return lax.cond(
        far[0] == 1,
        functools.partial(attend_and_project, places, requests, True),
        functools.partial(attend_and_project, places, requests, False),
        *(queries, keys, values, w_out, plan),
    )


def attend_and_project(places, requests, far, queries, keys, values, w_out, plan):
    ctx_count, head_count = lax.axis_size("ctx"), lax.axis_size("head")
    rows = queries.shape[0]
    cache, width = keys.shape
    heads = queries.shape[1] // width
    groups, chips, half = ctx_count // 2, head_count // 2, cache // 2
    core = lax.axis_index("head") % 2

    blocks = [move(queries, groups, steps, far) for steps in range(1, groups)]

    mine = [lax.dynamic_slice_in_dim(array, core * half, half, axis=0) for array in (keys, values)]
    got = lax.ppermute(jnp.concatenate(mine, axis=1), "ctx", swap_pairs(ctx_count))
    all_keys, beside, own_norm, near_w = prepare(keys, values, w_out)
    stack, query_norm = stack_queries(places, plan, [queries] + blocks, width)
    got, query_norm, own_norm = lax.optimization_barrier((got, query_norm, own_norm))
    rest = lax.ppermute(got, "head", swap_pairs(head_count))
    all_keys, beside, key_norm = join(got, rest, own_norm, all_keys, beside)

    parts = 2 if heads % 2 == 0 else 1
    few = heads // parts
    back = []
    for part in range(parts):
        sent = attend(
            places, plan, (key_norm, query_norm), stack, all_keys, beside, (groups, rows, requests), part * few, few
        )
        back.append([sent[0]] + [move(sent[steps], groups, groups - steps, far) for steps in range(1, groups)])
    mixed, pieces, token = None, [], jnp.zeros((1,), jnp.int32)
    for part, arrived in enumerate(back):
        arrived, pieces = lax.optimization_barrier((arrived, pieces))
        attended = merge(places, plan, arrived, rows, few)
        away = [lax.ppermute(attended, "head", shift_pairs(head_count, 2, steps)) for steps in range(1, chips)]
        pair = lax.ppermute(attended, "head", swap_pairs(head_count))
        if part:
            mixed, token = project(places, plan, pieces, parts, part - 1, mixed, near_w)
            away, token = lax.optimization_barrier((away, token))
        pieces = [attended] + away + [pair] + [lax.ppermute(piece, "head", swap_pairs(head_count)) for piece in away]
    mixed, _ = project(places, plan, pieces, parts, parts - 1, mixed, near_w)
    return mixed


def solution(mesh):
    return jax.shard_map(
        body,
        mesh=mesh,
        in_specs=(P("ctx", "head"), P("ctx", None), P("ctx", None), P(None, "head"), P(), P()),
        out_specs=P("ctx", "head"),
        check_vma=False,
    )
```

profile of v0, /device:TPU:0, one launch (start us, length us, event | category | flops | bytes accessed | tf_op | source)
XLA Modules:
  0.0 410.0 jit_solution(15638632269277280673)
XLA Ops:
  0.0 0.6 pad_add_fusion.at_ref
  0.6 1.4 plan.1
  2.7 407.3 %conditional.1 = (bf16[256,4096]{1,0:T(8,128)(2,1)}) conditional(s32[]{:T(128)} %bitcast.2, (bf16[4096,128]{1,0:T(8,128)(2,1)}, bf16[4096,128]{1,0:T(8,128)(2,1)}, bf16[256,512]{1,0:T(8,128)(2,1)}, s32[54]{0:T(128)S(1)}, bf16[2048,4096]{1,0:T(8,128)(2,1)}) %tuple.19, (bf16[4096,128]{1,0:T(8,128)(2,1)}, bf16[4096,128]{1,0:T(8,128)(2,1)}, ...), branch_computations={%region_0.1_spmd, %region_1.2_spmd} | conditional | flops 12886999040 | bytes 65209272 | solution.py:552
  2.9 0.0 copy-start.5
  3.0 0.0 copy-start.1
  3.0 0.0 copy-start.3
  3.0 1.4 constant_dynamic-slice_fusion.2
  4.4 0.1 pad_maximum_fusion.1
  4.5 3.0 collective-permute-start.17
  7.5 3.6 collective-permute-start.20
  11.1 0.0 collective-permute-start.19
  11.2 1.0 collective-permute-start.18
  12.2 6.3 %prepare.3 = (bf16[8192,128]{1,0:T(8,128)(2,1)S(1)}, bf16[8192,256]{1,0:T(8,128)(2,1)S(1)}, f32[1]{0:T(128)}, bf16[2048,4096]{1,0:T(8,128)(2,1)S(1)}) custom-call(bf16[4096,128]{1,0:T(8,128)(2,1)S(1)} %copy-done.1, bf16[4096,128]{1,0:T(8,128)(2,1)S(1)} %copy-done.3, bf16[2048,4096]{1,0:T(8,128)(2,1)} %get-tuple-element.72.far_w), custom_call_target="tpu_custom_call" | custom-call | tf_op jit(solution)/shard_map/cond/branch_1_fun/prepare/pallas_call | solution.py:58
  18.5 0.0 collective-permute-done.20.refs_3_
  18.5 14.7 %collective-permute-done.19.refs_2_ = bf16[256,512]{1,0:T(8,128)(2,1)S(1)} collective-permute-done((bf16[256,512]{1,0:T(8,128)(2,1)S(1)}, bf16[256,512]{1,0:T(8,128)(2,1)S(1)}, u32[]{:S(2)}, u32[]{:S(2)}) %collective-permute-start.19) | collective-permute-done | bytes 262176 | tf_op jit(solution)/shard_map/cond/branch_1_fun/ppermute | solution.py:472
  33.2 0.0 collective-permute-done.18.refs_1_
  33.2 2.3 stack.15
  35.5 0.0 collective-permute-done.17.got_ref
  35.5 0.1 collective-permute-start.21
  35.6 2.6 collective-permute-done.21.rest_ref
  38.2 3.1 join.3
  41.3 153.6 %attend.7 = (bf16[272,256]{1,0:T(8,128)(2,1)S(1)}, bf16[272,256]{1,0:T(8,128)(2,1)S(1)}, bf16[272,256]{1,0:T(8,128)(2,1)S(1)}, bf16[272,256]{1,0:T(8,128)(2,1)S(1)}) custom-call(s32[54]{0:T(128)S(1)} %get-tuple-element.67.plan_ref.refs_0_, f32[1]{0:T(128)} %get-tuple-element.78.refs_1_, f32[1]{0:T(128)} %get-tuple-element.79.refs_2_, ...), custom_call_target="tpu_custom_call" | custom-call | flops 4294967296 | bytes 8388608 | tf_op jit(solution)/shard_map/cond/branch_1_fun/attend/pallas_call | solution.py:335
  194.9 0.1 collective-permute-start.25
  195.0 11.1 %collective-permute-start.26 = (bf16[272,256]{1,0:T(8,128)(2,1)S(1)}, bf16[272,256]{1,0:T(8,128)(2,1)S(1)}, u32[]{:S(2)}, u32[]{:S(2)}) collective-permute-start(bf16[272,256]{1,0:T(8,128)(2,1)S(1)} %get-tuple-element.89), channel_id=1, source_target_pairs={{0,16},{4,20},{8,24},{12,28},{16,0},{20,4},{24,8},{28,12},{1,17},{... | collective-permute-start | bytes 417800 | tf_op jit(solution)/shard_map/cond/branch_1_fun/ppermute | solution.py:472
  206.1 0.0 collective-permute-start.27
  206.1 2.5 collective-permute-done.25.refs_1_
  208.6 10.1 %collective-permute-done.26.refs_2_ = bf16[272,256]{1,0:T(8,128)(2,1)S(1)} collective-permute-done((bf16[272,256]{1,0:T(8,128)(2,1)S(1)}, bf16[272,256]{1,0:T(8,128)(2,1)S(1)}, u32[]{:S(2)}, u32[]{:S(2)}) %collective-permute-start.26) | collective-permute-done | bytes 139296 | tf_op jit(solution)/shard_map/cond/branch_1_fun/ppermute | solution.py:472
  218.7 0.0 collective-permute-done.27.refs_3_
  218.7 1.5 merge.6.refs_0_
  220.3 1.6 collective-permute-start.28
  221.8 153.6 %attend.6 = (bf16[272,256]{1,0:T(8,128)(2,1)S(1)}, bf16[272,256]{1,0:T(8,128)(2,1)S(1)}, bf16[272,256]{1,0:T(8,128)(2,1)S(1)}, bf16[272,256]{1,0:T(8,128)(2,1)S(1)}) custom-call(s32[54]{0:T(128)S(1)} %get-tuple-element.67.plan_ref.refs_0_, f32[1]{0:T(128)} %get-tuple-element.78.refs_1_, f32[1]{0:T(128)} %get-tuple-element.79.refs_2_, ...), custom_call_target="tpu_custom_call" | custom-call | flops 4294967296 | bytes 8388608 | tf_op jit(solution)/shard_map/cond/branch_1_fun/attend/pallas_call | solution.py:335
  375.4 0.1 collective-permute-start.22
  375.5 8.6 %collective-permute-start.23 = (bf16[272,256]{1,0:T(8,128)(2,1)S(1)}, bf16[272,256]{1,0:T(8,128)(2,1)S(1)}, u32[]{:S(2)}, u32[]{:S(2)}) collective-permute-start(bf16[272,256]{1,0:T(8,128)(2,1)S(1)} %get-tuple-element.85), channel_id=1, source_target_pairs={{0,16},{4,20},{8,24},{12,28},{16,0},{20,4},{24,8},{28,12},{1,17},{... | collective-permute-start | bytes 417800 | tf_op jit(solution)/shard_map/cond/branch_1_fun/ppermute | solution.py:472
  384.1 0.0 collective-permute-start.24
  384.1 0.5 collective-permute-start.30
  384.6 1.1 collective-permute-done.22.refs_1_
  385.7 9.1 %collective-permute-done.23.refs_2_ = bf16[272,256]{1,0:T(8,128)(2,1)S(1)} collective-permute-done((bf16[272,256]{1,0:T(8,128)(2,1)S(1)}, bf16[272,256]{1,0:T(8,128)(2,1)S(1)}, u32[]{:S(2)}, u32[]{:S(2)}) %collective-permute-start.23) | collective-permute-done | bytes 139296 | tf_op jit(solution)/shard_map/cond/branch_1_fun/ppermute | solution.py:472
  394.8 0.0 collective-permute-done.24.refs_3_
  394.8 0.0 collective-permute-done.29.refs_2_
  394.8 0.0 collective-permute-done.30.refs_3_
  394.8 1.5 merge.7.refs_1_
  396.4 0.6 collective-permute-start.31
  396.9 0.0 collective-permute-start.32
  396.9 4.5 %collective-permute-done.31.refs_2_ = bf16[256,256]{1,0:T(8,128)(2,1)S(1)} collective-permute-done((bf16[256,256]{1,0:T(8,128)(2,1)S(1)}, bf16[256,256]{1,0:T(8,128)(2,1)S(1)}, u32[]{:S(2)}, u32[]{:S(2)}) %collective-permute-start.31) | collective-permute-done | bytes 131104 | tf_op jit(solution)/shard_map/cond/branch_1_fun/ppermute | solution.py:590
  401.4 0.0 collective-permute-start.33
  401.4 4.2 %project.6 = (f32[256,4096]{1,0:T(8,128)S(1)}, s32[1]{0:T(128)}) custom-call(s32[54]{0:T(128)S(1)} %get-tuple-element.67.plan_ref.refs_0_, bf16[256,256]{1,0:T(8,128)(2,1)S(1)} %merge.6.refs_0_, bf16[256,256]{1,0:T(8,128)(2,1)S(1)} %collective-permute-done.28.refs_1_, bf16[256,256]{1,0:T(8,128)(2,1)S(1)} %collective-permute-done.29.refs_2_, ...), custom_call_target="tpu_custom_call" | custom-call | flops 2147483648 | bytes 8388608 | tf_op jit(solution)/shard_map/cond/branch_1_fun/project/pallas_call | solution.py:431
  405.6 0.0 collective-permute-done.32.refs_3_
  405.7 4.4 %project.7 = (bf16[256,4096]{1,0:T(8,128)(2,1)}, s32[1]{0:T(128)}) custom-call(s32[54]{0:T(128)S(1)} %get-tuple-element.67.plan_ref.refs_0_, f32[256,4096]{1,0:T(8,128)S(1)} %get-tuple-element.100.refs_0_, bf16[256,256]{1,0:T(8,128)(2,1)S(1)} %merge.7.refs_1_, bf16[256,256]{1,0:T(8,128)(2,1)S(1)} %collective-permute-done.31.refs_2_, ...), custom_call_target="tpu_custom_call" | custom-call | flops 2147483648 | bytes 8388608 | tf_op jit(solution)/shard_map/cond/branch_1_fun/project/pallas_call | solution.py:431
  (6 shorter events, 0.0 us)
Async XLA Ops:
  2.9 4.6 %copy-start.5 = (bf16[256,512]{1,0:T(8,128)(2,1)S(1)}, bf16[256,512]{1,0:T(8,128)(2,1)}, u32[]{:S(2)}) copy-start(bf16[256,512]{1,0:T(8,128)(2,1)} %get-tuple-element.70.refs_0_) | copy-start | bytes 786436 | tf_op jit(solution)/shard_map/cond
  3.0 9.2 %copy-start.1 = (bf16[4096,128]{1,0:T(8,128)(2,1)S(1)}, bf16[4096,128]{1,0:T(8,128)(2,1)}, u32[]{:S(2)}) copy-start(bf16[4096,128]{1,0:T(8,128)(2,1)} %get-tuple-element.68.keys_ref) | copy-start | bytes 3145732 | tf_op jit(solution)/shard_map/cond
  3.0 9.2 %copy-start.3 = (bf16[4096,128]{1,0:T(8,128)(2,1)S(1)}, bf16[4096,128]{1,0:T(8,128)(2,1)}, u32[]{:S(2)}) copy-start(bf16[4096,128]{1,0:T(8,128)(2,1)} %get-tuple-element.69.values_ref) | copy-start | bytes 3145732 | tf_op jit(solution)/shard_map/cond
  4.5 30.9 %collective-permute-start.17 = (bf16[2048,256]{1,0:T(8,128)(2,1)S(1)}, bf16[2048,256]{1,0:T(8,128)(2,1)S(1)}, u32[]{:S(2)}, u32[]{:S(2)}) collective-permute-start(bf16[2048,256]{1,0:T(8,128)(2,1)S(1)} %pad_maximum_fusion.1), channel_id=1, source_target_pairs={{0,4},{4,0},{8,12},{12,8},{16,20},{20,16},{24,28},{28,24},{1,5},{5... | collective-permute-start | bytes 3145736 | tf_op jit(solution)/shard_map/cond/branch_1_fun/ppermute | solution.py:571
  7.5 10.9 %collective-permute-start.20 = (bf16[256,512]{1,0:T(8,128)(2,1)S(1)}, bf16[256,512]{1,0:T(8,128)(2,1)S(1)}, u32[]{:S(2)}, u32[]{:S(2)}) collective-permute-start(bf16[256,512]{1,0:T(8,128)(2,1)S(1)} %copy-done.5), channel_id=1, source_target_pairs={{0,24},{4,28},{8,0},{12,4},{16,8},{20,12},{24,16},{28,20},{1,25},{... | collective-permute-start | bytes 786440 | tf_op jit(solution)/shard_map/cond/branch_1_fun/ppermute | solution.py:472
  11.1 22.0 %collective-permute-start.19 = (bf16[256,512]{1,0:T(8,128)(2,1)S(1)}, bf16[256,512]{1,0:T(8,128)(2,1)S(1)}, u32[]{:S(2)}, u32[]{:S(2)}) collective-permute-start(bf16[256,512]{1,0:T(8,128)(2,1)S(1)} %copy-done.5), channel_id=1, source_target_pairs={{0,16},{4,20},{8,24},{12,28},{16,0},{20,4},{24,8},{28,12},{1,17},{... | collective-permute-start | bytes 786440 | tf_op jit(solution)/shard_map/cond/branch_1_fun/ppermute | solution.py:472
  11.2 22.0 %collective-permute-start.18 = (bf16[256,512]{1,0:T(8,128)(2,1)S(1)}, bf16[256,512]{1,0:T(8,128)(2,1)S(1)}, u32[]{:S(2)}, u32[]{:S(2)}) collective-permute-start(bf16[256,512]{1,0:T(8,128)(2,1)S(1)} %copy-done.5), channel_id=1, source_target_pairs={{0,8},{4,12},{8,16},{12,20},{16,24},{20,28},{24,0},{28,4},{1,9},{5... | collective-permute-start | bytes 786440 | tf_op jit(solution)/shard_map/cond/branch_1_fun/ppermute | solution.py:472
  35.5 2.7 collective-permute-start.21
  194.9 13.7 %collective-permute-start.25 = (bf16[272,256]{1,0:T(8,128)(2,1)S(1)}, bf16[272,256]{1,0:T(8,128)(2,1)S(1)}, u32[]{:S(2)}, u32[]{:S(2)}) collective-permute-start(bf16[272,256]{1,0:T(8,128)(2,1)S(1)} %get-tuple-element.88), channel_id=1, source_target_pairs={{0,24},{4,28},{8,0},{12,4},{16,8},{20,12},{24,16},{28,20},{1,25},{... | collective-permute-start | bytes 417800 | tf_op jit(solution)/shard_map/cond/branch_1_fun/ppermute | solution.py:472
  195.0 23.8 %collective-permute-start.26 = (bf16[272,256]{1,0:T(8,128)(2,1)S(1)}, bf16[272,256]{1,0:T(8,128)(2,1)S(1)}, u32[]{:S(2)}, u32[]{:S(2)}) collective-permute-start(bf16[272,256]{1,0:T(8,128)(2,1)S(1)} %get-tuple-element.89), channel_id=1, source_target_pairs={{0,16},{4,20},{8,24},{12,28},{16,0},{20,4},{24,8},{28,12},{1,17},{... | collective-permute-start | bytes 417800 | tf_op jit(solution)/shard_map/cond/branch_1_fun/ppermute | solution.py:472
  206.1 12.6 %collective-permute-start.27 = (bf16[272,256]{1,0:T(8,128)(2,1)S(1)}, bf16[272,256]{1,0:T(8,128)(2,1)S(1)}, u32[]{:S(2)}, u32[]{:S(2)}) collective-permute-start(bf16[272,256]{1,0:T(8,128)(2,1)S(1)} %get-tuple-element.90), channel_id=1, source_target_pairs={{0,8},{4,12},{8,16},{12,20},{16,24},{20,28},{24,0},{28,4},{1,9},{5... | collective-permute-start | bytes 417800 | tf_op jit(solution)/shard_map/cond/branch_1_fun/ppermute | solution.py:472
  220.3 163.9 %collective-permute-start.28 = (bf16[256,256]{1,0:T(8,128)(2,1)S(1)}, bf16[256,256]{1,0:T(8,128)(2,1)S(1)}, u32[]{:S(2)}, u32[]{:S(2)}) collective-permute-start(bf16[256,256]{1,0:T(8,128)(2,1)S(1)} %merge.6.refs_0_), channel_id=1, source_target_pairs={{0,2},{1,3},{2,0},{3,1},{4,6},{5,7},{6,4},{7,5},{8,10},{9,11},{10,... | collective-permute-start | bytes 393224 | tf_op jit(solution)/shard_map/cond/branch_1_fun/ppermute | solution.py:590
  375.4 10.3 %collective-permute-start.22 = (bf16[272,256]{1,0:T(8,128)(2,1)S(1)}, bf16[272,256]{1,0:T(8,128)(2,1)S(1)}, u32[]{:S(2)}, u32[]{:S(2)}) collective-permute-start(bf16[272,256]{1,0:T(8,128)(2,1)S(1)} %get-tuple-element.84), channel_id=1, source_target_pairs={{0,24},{4,28},{8,0},{12,4},{16,8},{20,12},{24,16},{28,20},{1,25},{... | collective-permute-start | bytes 417800 | tf_op jit(solution)/shard_map/cond/branch_1_fun/ppermute | solution.py:472
  375.5 19.4 %collective-permute-start.23 = (bf16[272,256]{1,0:T(8,128)(2,1)S(1)}, bf16[272,256]{1,0:T(8,128)(2,1)S(1)}, u32[]{:S(2)}, u32[]{:S(2)}) collective-permute-start(bf16[272,256]{1,0:T(8,128)(2,1)S(1)} %get-tuple-element.85), channel_id=1, source_target_pairs={{0,16},{4,20},{8,24},{12,28},{16,0},{20,4},{24,8},{28,12},{1,17},{... | collective-permute-start | bytes 417800 | tf_op jit(solution)/shard_map/cond/branch_1_fun/ppermute | solution.py:472
  384.1 10.7 %collective-permute-start.24 = (bf16[272,256]{1,0:T(8,128)(2,1)S(1)}, bf16[272,256]{1,0:T(8,128)(2,1)S(1)}, u32[]{:S(2)}, u32[]{:S(2)}) collective-permute-start(bf16[272,256]{1,0:T(8,128)(2,1)S(1)} %get-tuple-element.86), channel_id=1, source_target_pairs={{0,8},{4,12},{8,16},{12,20},{16,24},{20,28},{24,0},{28,4},{1,9},{5... | collective-permute-start | bytes 417800 | tf_op jit(solution)/shard_map/cond/branch_1_fun/ppermute | solution.py:472
  384.1 10.7 %collective-permute-start.29 = (bf16[256,256]{1,0:T(8,128)(2,1)S(1)}, bf16[256,256]{1,0:T(8,128)(2,1)S(1)}, u32[]{:S(2)}, u32[]{:S(2)}) collective-permute-start(bf16[256,256]{1,0:T(8,128)(2,1)S(1)} %merge.6.refs_0_), channel_id=1, source_target_pairs={{0,1},{1,0},{2,3},{3,2},{4,5},{5,4},{6,7},{7,6},{8,9},{9,8},{10,11... | collective-permute-start | bytes 393224 | tf_op jit(solution)/shard_map/cond/branch_1_fun/ppermute | solution.py:591
  384.1 10.7 %collective-permute-start.30 = (bf16[256,256]{1,0:T(8,128)(2,1)S(1)}, bf16[256,256]{1,0:T(8,128)(2,1)S(1)}, u32[]{:S(2)}, u32[]{:S(2)}) collective-permute-start(bf16[256,256]{1,0:T(8,128)(2,1)S(1)} %collective-permute-done.28.refs_1_), channel_id=1, source_target_pairs={{0,1},{1,0},{2,3},{3,2},{4,5},{5,4},{6,7},{7,6},{8,9},{9,8},{10,11... | collective-permute-start | bytes 393224 | tf_op jit(solution)/shard_map/cond/branch_1_fun/ppermute | solution.py:595
  396.4 5.0 %collective-permute-start.31 = (bf16[256,256]{1,0:T(8,128)(2,1)S(1)}, bf16[256,256]{1,0:T(8,128)(2,1)S(1)}, u32[]{:S(2)}, u32[]{:S(2)}) collective-permute-start(bf16[256,256]{1,0:T(8,128)(2,1)S(1)} %merge.7.refs_1_), channel_id=1, source_target_pairs={{0,2},{1,3},{2,0},{3,1},{4,6},{5,7},{6,4},{7,5},{8,10},{9,11},{10,... | collective-permute-start | bytes 393224 | tf_op jit(solution)/shard_map/cond/branch_1_fun/ppermute | solution.py:590
  396.9 8.7 %collective-permute-start.32 = (bf16[256,256]{1,0:T(8,128)(2,1)S(1)}, bf16[256,256]{1,0:T(8,128)(2,1)S(1)}, u32[]{:S(2)}, u32[]{:S(2)}) collective-permute-start(bf16[256,256]{1,0:T(8,128)(2,1)S(1)} %merge.7.refs_1_), channel_id=1, source_target_pairs={{0,1},{1,0},{2,3},{3,2},{4,5},{5,4},{6,7},{7,6},{8,9},{9,8},{10,11... | collective-permute-start | bytes 393224 | tf_op jit(solution)/shard_map/cond/branch_1_fun/ppermute | solution.py:591
  401.4 4.3 %collective-permute-start.33 = (bf16[256,256]{1,0:T(8,128)(2,1)S(1)}, bf16[256,256]{1,0:T(8,128)(2,1)S(1)}, u32[]{:S(2)}, u32[]{:S(2)}) collective-permute-start(bf16[256,256]{1,0:T(8,128)(2,1)S(1)} %collective-permute-done.31.refs_2_), channel_id=1, source_target_pairs={{0,1},{1,0},{2,3},{3,2},{4,5},{5,4},{6,7},{7,6},{8,9},{9,8},{10,11... | collective-permute-start | bytes 393224 | tf_op jit(solution)/shard_map/cond/branch_1_fun/ppermute | solution.py:595
where the time goes:
time: 411 us; the launch traced here: 410 us
  Pallas kernels  332 us (81%)
  waiting for transfers between devices  44.6 us (11%)
  starting transfers between devices  30.3 us (7%)
    pallas_call x2, Pallas kernels, attend(): pl.pallas_call(functools.partial(attend_kernel, (*shape, many), dict(plac...  307 us
    ppermute x9, waiting for transfers between devices, move(): return lax.ppermute(value, 'ctx', pairs) if pairs else jnp.zeros_like(value)  37.5 us
    ppermute x9, starting transfers between devices, move(): return lax.ppermute(value, 'ctx', pairs) if pairs else jnp.zeros_like(value)  24.5 us
    pallas_call x2, Pallas kernels, project(): pl.pallas_call(functools.partial(project_kernel, len(pieces), parts, part...  8.6 us
  transfers between devices with their start and end apart: 17, of which 7 were waited for; matrix products, arithmetic and copies ran while one was open for 0% of the time, Pallas kernels for 41%

commit v1 on v0

--- a/solution.py
+++ b/solution.py
@@ -13,7 +13,6 @@
 KEY_TILE = 512
 FEW_ROWS = 64
 SIDE = 16
-SLACK = 1.05
 LANES = 128
 MIB = 1024 * 1024
 SMEM = pl.BlockSpec(memory_space=pltpu.SMEM)
@@ -23,13 +22,12 @@
 
 def lengths(rows):
     wide = rows.astype(jnp.float32)
-    ones = jnp.ones((rows.shape[1], LANES), jnp.bfloat16)
-    return jnp.dot((wide * wide).astype(jnp.bfloat16), ones, preferred_element_type=jnp.float32)
+    return jnp.sum(wide * wide, axis=1, keepdims=True)
 
 
 def fill(parts, keys_ref, beside_ref):
     width = keys_ref.shape[1]
-    longest = jnp.zeros((KEY_TILE, LANES), jnp.float32)
+    longest = jnp.zeros((min(KEY_TILE, parts[0][0].shape[0]), 1), jnp.float32)
     for from_keys, from_values, done in parts:
         step = min(KEY_TILE, from_keys.shape[0])
 
@@ -104,7 +102,7 @@
     copies = [pltpu.make_async_copy(q_ref, q_all.at[slot], sems.at[slot]) for slot, q_ref in enumerate(q_refs)]
     for copy in copies:
         copy.start()
-    longest = jnp.zeros((rows, LANES), jnp.float32)
+    longest = jnp.zeros((rows, 1), jnp.float32)
     for slot, copy in enumerate(copies):
         copy.wait()
         start = plan_ref[group_at + slot] * rows
@@ -160,7 +158,7 @@
     step = min(KEY_TILE, keys_ref.shape[0] // 4)
     scale = width ** (-0.5)
     factor = scale * math.log2(math.e)
-    calm = key_norm_ref[0] * query_norm_ref[0] * (SLACK * scale * scale) <= CALM * CALM
+    calm = key_norm_ref[0] * query_norm_ref[0] * (scale * scale) <= CALM * CALM
     side = plan_ref[places["side"]]
 
     def clear(at, carry):
@@ -195,7 +193,7 @@
             return lax.dot_general(
                 chunk_q[part, :], keys_ref[pl.ds(left, step), :], (((1,), (1,)), ((), ())),
                 preferred_element_type=jnp.float32,
-            ) * factor
+            )
 
         def add(left, weights):
             return jnp.dot(
@@ -212,7 +210,7 @@
 
                 def one_head(head, carry):
                     part = pl.ds(pl.multiple_of(head * count, count), count)
-                    score = jnp.where(mask, scores(part, left), NEG)
+                    score = jnp.where(mask, scores(part, left) * factor, NEG)
                     old = chunk_top[part, :]
                     new = jnp.maximum(old, jnp.ceil(jnp.max(score, axis=1, keepdims=True)))
                     weights = jnp.where(mask, jnp.exp2(score - new[:, :1]), 0.0)
@@ -230,12 +228,12 @@
 
             @pl.when(plain)
             def _():
-                chunk_sum[:total, :] += add(left, jnp.exp2(scores(pl.ds(0, total), left)))
+                chunk_sum[:total, :] += add(left, jnp.exp(scores(pl.ds(0, total), left) * scale))
 
             @pl.when(jnp.logical_not(plain))
             def _():
                 mask = allowed()
-                weights = jnp.exp2(scores(pl.ds(0, total), left))
+                weights = jnp.exp(scores(pl.ds(0, total), left) * scale)
                 weights = jnp.concatenate([
                     jnp.where(mask, weights[head * count:(head + 1) * count, :], 0.0) for head in range(heads)
                 ])
@@ -346,7 +344,7 @@
         ],
         compiler_params=pltpu.CompilerParams(vmem_limit_bytes=20 * MIB),
         cost_estimate=pl.CostEstimate(
-            flops=local * heads * keys.shape[0] * width * 2, bytes_accessed=8 * MIB, transcendentals=0
+            flops=local * heads * keys.shape[0] * width * 12, bytes_accessed=8 * MIB, transcendentals=0
         ),
         name="attend",
     )(plan, *norms, stack, keys, beside)
@@ -583,6 +581,7 @@
             places, plan, (key_norm, query_norm), stack, all_keys, beside, (groups, rows, requests), part * few, few
         )
         back.append([sent[0]] + [move(sent[steps], groups, groups - steps, far) for steps in range(1, groups)])
+    back[0], back[-1][0] = lax.optimization_barrier((back[0], back[-1][0]))
     mixed, pieces, token = None, [], jnp.zeros((1,), jnp.int32)
     for part, arrived in enumerate(back):
         arrived, pieces = lax.optimization_barrier((arrived, pieces))

time: 411 us -> 400 us (0.973)
  waiting for transfers between devices: 44.6 us -> 16.8 us
  starting transfers between devices: 30.3 us -> 41 us
  Pallas kernels: 332 us -> 338 us
    ppermute x9, waiting for transfers between devices: 37.5 us -> 6.18 us  [move(): return lax.ppermute(value, 'ctx', pairs) if pairs else jnp.zeros_like(value)]
    ppermute x9, starting transfers between devices: 24.5 us -> 35.3 us  [move(): return lax.ppermute(value, 'ctx', pairs) if pairs else jnp.zeros_like(value)]
    pallas_call x2, Pallas kernels: 307 us -> 314 us  [attend(): pl.pallas_call(functools.partial(attend_kernel, (*shape, many), dict(plac...]
  transfers between devices with their start and end apart: 17 -> 17, of which waited for: 7 -> 7; matrix products, arithmetic and copies ran while one was open for 0% -> 0% of each run, Pallas kernels for 41% -> 42%
where the time goes in v1:
time: 400 us; the launch traced here: 399 us
  Pallas kernels  338 us (84%)
  starting transfers between devices  41 us (10%)
  waiting for transfers between devices  16.8 us (4%)
    pallas_call x2, Pallas kernels, attend(): pl.pallas_call(functools.partial(attend_kernel, (*shape, many), dict(plac...  314 us
    ppermute x9, starting transfers between devices, move(): return lax.ppermute(value, 'ctx', pairs) if pairs else jnp.zeros_like(value)  35.3 us
    pallas_call x2, Pallas kernels, project(): pl.pallas_call(functools.partial(project_kernel, len(pieces), parts, part...  8.59 us
  transfers between devices with their start and end apart: 17, of which 7 were waited for; matrix products, arithmetic and copies ran while one was open for 0% of the time, Pallas kernels for 42%

profile of v1, /device:TPU:0, one launch (start us, length us, event | category | flops | bytes accessed | tf_op | source)
XLA Modules:
  0.0 399.2 jit_solution(11939212474741515586)
XLA Ops:
  0.0 0.6 pad_add_fusion.at_ref
  0.6 1.4 plan.1
  2.7 396.5 %conditional.1 = (bf16[256,4096]{1,0:T(8,128)(2,1)}) conditional(s32[]{:T(128)} %bitcast.2, (bf16[4096,128]{1,0:T(8,128)(2,1)}, bf16[4096,128]{1,0:T(8,128)(2,1)}, bf16[256,512]{1,0:T(8,128)(2,1)}, s32[54]{0:T(128)S(1)}, bf16[2048,4096]{1,0:T(8,128)(2,1)}) %tuple.21, (bf16[4096,128]{1,0:T(8,128)(2,1)}, bf16[4096,128]{1,0:T(8,128)(2,1)}, ...), branch_computations={%region_0.1_spmd, %region_1.2_spmd} | conditional | flops 55836672000 | bytes 65209272 | solution.py:550
  2.8 0.0 copy-start.4
  2.8 0.0 copy-start
  2.8 0.0 copy-start.2
  2.8 1.4 constant_dynamic-slice_fusion
  4.2 0.1 pad_maximum_fusion
  4.3 3.0 collective-permute-start
  7.4 1.3 collective-permute-start.3
  8.6 5.6 %collective-permute-start.2 = (bf16[256,512]{1,0:T(8,128)(2,1)S(1)}, bf16[256,512]{1,0:T(8,128)(2,1)S(1)}, u32[]{:S(2)}, u32[]{:S(2)}) collective-permute-start(bf16[256,512]{1,0:T(8,128)(2,1)S(1)} %copy-done.4), channel_id=1, source_target_pairs={{0,16},{4,20},{16,0},{20,4},{1,17},{5,21},{17,1},{21,5},{2,18},{6,... | collective-permute-start | bytes 786440 | tf_op jit(solution)/shard_map/cond/branch_0_fun/ppermute | solution.py:470
  14.2 1.3 collective-permute-start.1
  15.6 6.3 %prepare.2 = (bf16[8192,128]{1,0:T(8,128)(2,1)S(1)}, bf16[8192,256]{1,0:T(8,128)(2,1)S(1)}, f32[1]{0:T(128)}, bf16[2048,4096]{1,0:T(8,128)(2,1)S(1)}) custom-call(bf16[4096,128]{1,0:T(8,128)(2,1)S(1)} %copy-done, bf16[4096,128]{1,0:T(8,128)(2,1)S(1)} %copy-done.2, bf16[2048,4096]{1,0:T(8,128)(2,1)} %get-tuple-element.33.far_w), custom_call_target="tpu_custom_call" | custom-call | tf_op jit(solution)/shard_map/cond/branch_0_fun/prepare/pallas_call | solution.py:56
  21.9 0.0 collective-permute-done.3.refs_3_
  21.9 1.8 collective-permute-done.2.refs_2_
  23.6 1.2 collective-permute-done.1.refs_1_
  24.9 2.1 stack.14
  27.0 3.5 collective-permute-done.got_ref
  30.5 0.0 collective-permute-start.4
  30.5 2.7 collective-permute-done.4.rest_ref
  33.2 2.8 join.2
  36.0 157.0 %attend.4 = (bf16[272,256]{1,0:T(8,128)(2,1)S(1)}, bf16[272,256]{1,0:T(8,128)(2,1)S(1)}, bf16[272,256]{1,0:T(8,128)(2,1)S(1)}, bf16[272,256]{1,0:T(8,128)(2,1)S(1)}) custom-call(s32[54]{0:T(128)S(1)} %get-tuple-element.28.plan_ref.refs_0_, f32[1]{0:T(128)} %get-tuple-element.39.refs_1_, f32[1]{0:T(128)} %get-tuple-element.40.refs_2_, ...), custom_call_target="tpu_custom_call" | custom-call | flops 25769803776 | bytes 8388608 | tf_op jit(solution)/shard_map/cond/branch_0_fun/attend/pallas_call | solution.py:333
  193.0 1.3 collective-permute-start.5
  194.3 11.3 %collective-permute-start.6 = (bf16[272,256]{1,0:T(8,128)(2,1)S(1)}, bf16[272,256]{1,0:T(8,128)(2,1)S(1)}, u32[]{:S(2)}, u32[]{:S(2)}) collective-permute-start(bf16[272,256]{1,0:T(8,128)(2,1)S(1)} %get-tuple-element.46), channel_id=1, source_target_pairs={{0,16},{4,20},{16,0},{20,4},{1,17},{5,21},{17,1},{21,5},{2,18},{6,... | collective-permute-start | bytes 417800 | tf_op jit(solution)/shard_map/cond/branch_0_fun/ppermute | solution.py:470
  205.6 1.3 collective-permute-start.7
  206.9 157.0 %attend.5 = (bf16[272,256]{1,0:T(8,128)(2,1)S(1)}, bf16[272,256]{1,0:T(8,128)(2,1)S(1)}, bf16[272,256]{1,0:T(8,128)(2,1)S(1)}, bf16[272,256]{1,0:T(8,128)(2,1)S(1)}) custom-call(s32[54]{0:T(128)S(1)} %get-tuple-element.28.plan_ref.refs_0_, f32[1]{0:T(128)} %get-tuple-element.39.refs_1_, f32[1]{0:T(128)} %get-tuple-element.40.refs_2_, ...), custom_call_target="tpu_custom_call" | custom-call | flops 25769803776 | bytes 8388608 | tf_op jit(solution)/shard_map/cond/branch_0_fun/attend/pallas_call | solution.py:333
  363.9 0.0 collective-permute-done.5.refs_1_
  363.9 0.0 collective-permute-done.6.refs_2_
  363.9 0.0 collective-permute-done.7.refs_3_
  363.9 1.5 merge.4.refs_0_
  365.4 1.6 collective-permute-start.11
  367.0 1.3 collective-permute-start.8
  368.3 10.7 %collective-permute-start.9 = (bf16[272,256]{1,0:T(8,128)(2,1)S(1)}, bf16[272,256]{1,0:T(8,128)(2,1)S(1)}, u32[]{:S(2)}, u32[]{:S(2)}) collective-permute-start(bf16[272,256]{1,0:T(8,128)(2,1)S(1)} %get-tuple-element.51), channel_id=1, source_target_pairs={{0,16},{4,20},{16,0},{20,4},{1,17},{5,21},{17,1},{21,5},{2,18},{6,... | collective-permute-start | bytes 417800 | tf_op jit(solution)/shard_map/cond/branch_0_fun/ppermute | solution.py:470
  379.0 1.3 collective-permute-start.10
  380.3 0.1 collective-permute-start.12
  380.4 0.0 collective-permute-done.11.refs_1_
  380.4 0.5 collective-permute-start.13
  380.9 0.0 collective-permute-done.8.refs_1_
  380.9 2.2 collective-permute-done.9.refs_2_
  383.1 1.0 collective-permute-done.10.refs_3_
  384.1 0.0 collective-permute-done.12.refs_2_
  384.1 0.0 collective-permute-done.13.refs_3_
  384.1 1.5 merge.5.refs_1_
  385.6 0.6 collective-permute-start.14
  386.1 0.0 collective-permute-start.15
  386.2 4.5 %collective-permute-done.14.refs_2_ = bf16[256,256]{1,0:T(8,128)(2,1)S(1)} collective-permute-done((bf16[256,256]{1,0:T(8,128)(2,1)S(1)}, bf16[256,256]{1,0:T(8,128)(2,1)S(1)}, u32[]{:S(2)}, u32[]{:S(2)}) %collective-permute-start.14) | collective-permute-done | bytes 131104 | tf_op jit(solution)/shard_map/cond/branch_0_fun/ppermute | solution.py:589
  390.6 4.2 %project.4 = (f32[256,4096]{1,0:T(8,128)S(1)}, s32[1]{0:T(128)}) custom-call(s32[54]{0:T(128)S(1)} %get-tuple-element.28.plan_ref.refs_0_, bf16[256,256]{1,0:T(8,128)(2,1)S(1)} %merge.4.refs_0_, bf16[256,256]{1,0:T(8,128)(2,1)S(1)} %collective-permute-done.11.refs_1_, bf16[256,256]{1,0:T(8,128)(2,1)S(1)} %collective-permute-done.12.refs_2_, ...), custom_call_target="tpu_custom_call" | custom-call | flops 2147483648 | bytes 8388608 | tf_op jit(solution)/shard_map/cond/branch_0_fun/project/pallas_call | solution.py:429
  394.9 4.4 %project.5 = (bf16[256,4096]{1,0:T(8,128)(2,1)}, s32[1]{0:T(128)}) custom-call(s32[54]{0:T(128)S(1)} %get-tuple-element.28.plan_ref.refs_0_, f32[256,4096]{1,0:T(8,128)S(1)} %get-tuple-element.66.refs_0_, bf16[256,256]{1,0:T(8,128)(2,1)S(1)} %merge.5.refs_1_, bf16[256,256]{1,0:T(8,128)(2,1)S(1)} %collective-permute-done.14.refs_2_, ...), custom_call_target="tpu_custom_call" | custom-call | flops 2147483648 | bytes 8388608 | tf_op jit(solution)/shard_map/cond/branch_0_fun/project/pallas_call | solution.py:429
  (6 shorter events, 0.0 us)
Async XLA Ops:
  2.8 4.6 %copy-start.4 = (bf16[256,512]{1,0:T(8,128)(2,1)S(1)}, bf16[256,512]{1,0:T(8,128)(2,1)}, u32[]{:S(2)}) copy-start(bf16[256,512]{1,0:T(8,128)(2,1)} %get-tuple-element.31.refs_0_) | copy-start | bytes 786436 | tf_op jit(solution)/shard_map/cond
  2.8 12.8 %copy-start = (bf16[4096,128]{1,0:T(8,128)(2,1)S(1)}, bf16[4096,128]{1,0:T(8,128)(2,1)}, u32[]{:S(2)}) copy-start(bf16[4096,128]{1,0:T(8,128)(2,1)} %get-tuple-element.29.keys_ref) | copy-start | bytes 3145732 | tf_op jit(solution)/shard_map/cond
  2.8 12.8 %copy-start.2 = (bf16[4096,128]{1,0:T(8,128)(2,1)S(1)}, bf16[4096,128]{1,0:T(8,128)(2,1)}, u32[]{:S(2)}) copy-start(bf16[4096,128]{1,0:T(8,128)(2,1)} %get-tuple-element.30.values_ref) | copy-start | bytes 3145732 | tf_op jit(solution)/shard_map/cond
  4.3 26.2 %collective-permute-start = (bf16[2048,256]{1,0:T(8,128)(2,1)S(1)}, bf16[2048,256]{1,0:T(8,128)(2,1)S(1)}, u32[]{:S(2)}, u32[]{:S(2)}) collective-permute-start(bf16[2048,256]{1,0:T(8,128)(2,1)S(1)} %pad_maximum_fusion), channel_id=1, source_target_pairs={{0,4},{4,0},{8,12},{12,8},{16,20},{20,16},{24,28},{28,24},{1,5},{5... | collective-permute-start | bytes 3145736 | tf_op jit(solution)/shard_map/cond/branch_0_fun/ppermute | solution.py:569
  7.4 14.5 %collective-permute-start.3 = (bf16[256,512]{1,0:T(8,128)(2,1)S(1)}, bf16[256,512]{1,0:T(8,128)(2,1)S(1)}, u32[]{:S(2)}, u32[]{:S(2)}) collective-permute-start(bf16[256,512]{1,0:T(8,128)(2,1)S(1)} %copy-done.4), channel_id=1, source_target_pairs={{8,0},{12,4},{16,8},{20,12},{24,16},{28,20},{9,1},{13,5},{17,9},{2... | collective-permute-start | bytes 786440 | tf_op jit(solution)/shard_map/cond/branch_0_fun/ppermute | solution.py:470
  8.6 15.0 %collective-permute-start.2 = (bf16[256,512]{1,0:T(8,128)(2,1)S(1)}, bf16[256,512]{1,0:T(8,128)(2,1)S(1)}, u32[]{:S(2)}, u32[]{:S(2)}) collective-permute-start(bf16[256,512]{1,0:T(8,128)(2,1)S(1)} %copy-done.4), channel_id=1, source_target_pairs={{0,16},{4,20},{16,0},{20,4},{1,17},{5,21},{17,1},{21,5},{2,18},{6,... | collective-permute-start | bytes 786440 | tf_op jit(solution)/shard_map/cond/branch_0_fun/ppermute | solution.py:470
  14.2 10.6 %collective-permute-start.1 = (bf16[256,512]{1,0:T(8,128)(2,1)S(1)}, bf16[256,512]{1,0:T(8,128)(2,1)S(1)}, u32[]{:S(2)}, u32[]{:S(2)}) collective-permute-start(bf16[256,512]{1,0:T(8,128)(2,1)S(1)} %copy-done.4), channel_id=1, source_target_pairs={{0,8},{4,12},{8,16},{12,20},{16,24},{20,28},{1,9},{5,13},{9,17},{1... | collective-permute-start | bytes 786440 | tf_op jit(solution)/shard_map/cond/branch_0_fun/ppermute | solution.py:470
  30.5 2.7 collective-permute-start.4
  193.0 170.9 %collective-permute-start.5 = (bf16[272,256]{1,0:T(8,128)(2,1)S(1)}, bf16[272,256]{1,0:T(8,128)(2,1)S(1)}, u32[]{:S(2)}, u32[]{:S(2)}) collective-permute-start(bf16[272,256]{1,0:T(8,128)(2,1)S(1)} %get-tuple-element.45), channel_id=1, source_target_pairs={{8,0},{12,4},{16,8},{20,12},{24,16},{28,20},{9,1},{13,5},{17,9},{2... | collective-permute-start | bytes 417800 | tf_op jit(solution)/shard_map/cond/branch_0_fun/ppermute | solution.py:470
  194.3 169.6 %collective-permute-start.6 = (bf16[272,256]{1,0:T(8,128)(2,1)S(1)}, bf16[272,256]{1,0:T(8,128)(2,1)S(1)}, u32[]{:S(2)}, u32[]{:S(2)}) collective-permute-start(bf16[272,256]{1,0:T(8,128)(2,1)S(1)} %get-tuple-element.46), channel_id=1, source_target_pairs={{0,16},{4,20},{16,0},{20,4},{1,17},{5,21},{17,1},{21,5},{2,18},{6,... | collective-permute-start | bytes 417800 | tf_op jit(solution)/shard_map/cond/branch_0_fun/ppermute | solution.py:470
  205.6 158.3 %collective-permute-start.7 = (bf16[272,256]{1,0:T(8,128)(2,1)S(1)}, bf16[272,256]{1,0:T(8,128)(2,1)S(1)}, u32[]{:S(2)}, u32[]{:S(2)}) collective-permute-start(bf16[272,256]{1,0:T(8,128)(2,1)S(1)} %get-tuple-element.47), channel_id=1, source_target_pairs={{0,8},{4,12},{8,16},{12,20},{16,24},{20,28},{1,9},{5,13},{9,17},{1... | collective-permute-start | bytes 417800 | tf_op jit(solution)/shard_map/cond/branch_0_fun/ppermute | solution.py:470
  365.4 14.9 %collective-permute-start.11 = (bf16[256,256]{1,0:T(8,128)(2,1)S(1)}, bf16[256,256]{1,0:T(8,128)(2,1)S(1)}, u32[]{:S(2)}, u32[]{:S(2)}) collective-permute-start(bf16[256,256]{1,0:T(8,128)(2,1)S(1)} %merge.4.refs_0_), channel_id=1, source_target_pairs={{0,2},{1,3},{2,0},{3,1},{4,6},{5,7},{6,4},{7,5},{8,10},{9,11},{10,... | collective-permute-start | bytes 393224 | tf_op jit(solution)/shard_map/cond/branch_0_fun/ppermute | solution.py:589
  367.0 13.8 %collective-permute-start.8 = (bf16[272,256]{1,0:T(8,128)(2,1)S(1)}, bf16[272,256]{1,0:T(8,128)(2,1)S(1)}, u32[]{:S(2)}, u32[]{:S(2)}) collective-permute-start(bf16[272,256]{1,0:T(8,128)(2,1)S(1)} %get-tuple-element.50), channel_id=1, source_target_pairs={{8,0},{12,4},{16,8},{20,12},{24,16},{28,20},{9,1},{13,5},{17,9},{2... | collective-permute-start | bytes 417800 | tf_op jit(solution)/shard_map/cond/branch_0_fun/ppermute | solution.py:470
  368.3 14.7 %collective-permute-start.9 = (bf16[272,256]{1,0:T(8,128)(2,1)S(1)}, bf16[272,256]{1,0:T(8,128)(2,1)S(1)}, u32[]{:S(2)}, u32[]{:S(2)}) collective-permute-start(bf16[272,256]{1,0:T(8,128)(2,1)S(1)} %get-tuple-element.51), channel_id=1, source_target_pairs={{0,16},{4,20},{16,0},{20,4},{1,17},{5,21},{17,1},{21,5},{2,18},{6,... | collective-permute-start | bytes 417800 | tf_op jit(solution)/shard_map/cond/branch_0_fun/ppermute | solution.py:470
  379.0 5.1 %collective-permute-start.10 = (bf16[272,256]{1,0:T(8,128)(2,1)S(1)}, bf16[272,256]{1,0:T(8,128)(2,1)S(1)}, u32[]{:S(2)}, u32[]{:S(2)}) collective-permute-start(bf16[272,256]{1,0:T(8,128)(2,1)S(1)} %get-tuple-element.52), channel_id=1, source_target_pairs={{0,8},{4,12},{8,16},{12,20},{16,24},{20,28},{1,9},{5,13},{9,17},{1... | collective-permute-start | bytes 417800 | tf_op jit(solution)/shard_map/cond/branch_0_fun/ppermute | solution.py:470
  380.3 3.8 collective-permute-start.12
  380.4 3.7 collective-permute-start.13
  385.6 5.0 %collective-permute-start.14 = (bf16[256,256]{1,0:T(8,128)(2,1)S(1)}, bf16[256,256]{1,0:T(8,128)(2,1)S(1)}, u32[]{:S(2)}, u32[]{:S(2)}) collective-permute-start(bf16[256,256]{1,0:T(8,128)(2,1)S(1)} %merge.5.refs_1_), channel_id=1, source_target_pairs={{0,2},{1,3},{2,0},{3,1},{4,6},{5,7},{6,4},{7,5},{8,10},{9,11},{10,... | collective-permute-start | bytes 393224 | tf_op jit(solution)/shard_map/cond/branch_0_fun/ppermute | solution.py:589
  386.1 8.7 %collective-permute-start.15 = (bf16[256,256]{1,0:T(8,128)(2,1)S(1)}, bf16[256,256]{1,0:T(8,128)(2,1)S(1)}, u32[]{:S(2)}, u32[]{:S(2)}) collective-permute-start(bf16[256,256]{1,0:T(8,128)(2,1)S(1)} %merge.5.refs_1_), channel_id=1, source_target_pairs={{0,1},{1,0},{2,3},{3,2},{4,5},{5,4},{6,7},{7,6},{8,9},{9,8},{10,11... | collective-permute-start | bytes 393224 | tf_op jit(solution)/shard_map/cond/branch_0_fun/ppermute | solution.py:590
  390.6 4.3 %collective-permute-start.16 = (bf16[256,256]{1,0:T(8,128)(2,1)S(1)}, bf16[256,256]{1,0:T(8,128)(2,1)S(1)}, u32[]{:S(2)}, u32[]{:S(2)}) collective-permute-start(bf16[256,256]{1,0:T(8,128)(2,1)S(1)} %collective-permute-done.14.refs_2_), channel_id=1, source_target_pairs={{0,1},{1,0},{2,3},{3,2},{4,5},{5,4},{6,7},{7,6},{8,9},{9,8},{10,11... | collective-permute-start | bytes 393224 | tf_op jit(solution)/shard_map/cond/branch_0_fun/ppermute | solution.py:594
